TPU v7x, 32 devices: a whole 2x2x4 slice. The times are simulated.
32 devices in a mesh: gx: 16 (over z, y, x), gy: 2 (over core).
Axes of the slice: x: 2, y: 2, z: 4, core: 2. Of those that a mesh axis runs over, the one named last changes fastest.
Arguments:
- state: float32 [6, 256, 6144], P(None, 'gx', 'gy'), as said below
- shock_height: float32 [256, 32], P('gx'), may hold values from 0.9 to 1.1
- wall_segment: int32 [256], P('gx'), may hold values from 0 to 15, never falling along the last dimension, each value on 1 to 32 neighbouring positions
- segment_level: int32 [16], replicated, may hold values from 0 to 15
- blow_table: float32 [16, 32], replicated, may hold values from 0.1 to 1.5
Outputs:
- state_new: float32 [6, 256, 6144], P(None, 'gx', 'gy')
- shock_new: float32 [256, 32], P('gx')
Inputs may be any that keep to these rules, and one draw needn't show every extreme that they name: `state`: each cell has density in [0.5, 2], p / density in [0.6, 2.5], q5 / density in [0.05, 0.6], u in [0, 2], v and w in [-1, 1]. `wall_segment`: segment numbers never fall along the stream; each segment covers 1 to 32 cells.
All inputs are finite; a program needn't handle non-finite values.
Results may differ from a plain program's by a relative error of at most 0.00002.
Values sent between devices are 32-bit elements; how exact they have to be, the bound alone decides.
A program may use at most 64 MiB of HBM per device.

v0:
```python
import math

import jax
import jax.numpy as jnp
from jax import lax
from jax.sharding import PartitionSpec as P

HEAT_RATIO = 1.4
STREAM_STEP = 0.05
SPAN_STEP = 0.05
STRETCH_RATE = 2.0
CHARACTER_KELVIN = 3.0
WHITE_LAW_FACTOR = 1.0
LANDAU_TELLER = 0.002
FREE_PRESSURE = 0.1
FREE_MACH = 6.0
COURANT = 0.05


def padded(block, sides, width):
    for axis, dim in sides:
        count = lax.axis_size(axis)
        forward = [(i, i + 1) for i in range(count - 1)]
        backward = [(target, source) for source, target in forward]
        low = lax.ppermute(
            lax.slice_in_dim(block, block.shape[dim] - width, None, axis=dim), axis, forward
        )
        high = lax.ppermute(lax.slice_in_dim(block, 0, width, axis=dim), axis, backward)
        block = jnp.concatenate([low, block, high], axis=dim)
    return block


def broadcast(array, axis, root):
    mine = lax.axis_index(axis) == root
    return lax.psum(jnp.where(mine, array, jnp.zeros_like(array)), axis)


def zshift(values, offset, planes):
    length = values.shape[-1]
    plane_at = jnp.arange(length, dtype=jnp.int32) % planes
    if offset > 0:
        return jnp.where(
            plane_at >= offset,
            jnp.roll(values, offset, axis=-1),
            jnp.roll(values, offset - planes, axis=-1),
        )
    return jnp.where(
        plane_at < planes + offset,
        jnp.roll(values, offset, axis=-1),
        jnp.roll(values, offset + planes, axis=-1),
    )


def primitives(conserved):
    specific_volume_inverse = conserved[0]
    vel_x = conserved[1] / specific_volume_inverse
    vel_y = conserved[2] / specific_volume_inverse
    vel_z = conserved[3] / specific_volume_inverse
    thermodynamic_stress = (HEAT_RATIO - 1.0) * (
        conserved[4]
        - 0.5 * (conserved[1] * vel_x + conserved[2] * vel_y + conserved[3] * vel_z)
        - conserved[5]
    )
    sound_speed = jnp.sqrt(HEAT_RATIO * thermodynamic_stress / specific_volume_inverse)
    return (specific_volume_inverse, vel_x, vel_y, vel_z, thermodynamic_stress, sound_speed)


def face_difference(plus_flux, minus_flux, cells, axis_at, stride):

    def window(values, offset):
        return lax.slice_in_dim(
            values, offset * stride, (offset + cells + 1) * stride, axis=axis_at
        )

    upwind = (
        2.0 * window(plus_flux, 0)
        - 13.0 * window(plus_flux, 1)
        + 47.0 * window(plus_flux, 2)
        + 27.0 * window(plus_flux, 3)
        - 3.0 * window(plus_flux, 4)
    ) / 60.0
    downwind = (
        -3.0 * window(minus_flux, 1)
        + 27.0 * window(minus_flux, 2)
        + 47.0 * window(minus_flux, 3)
        - 13.0 * window(minus_flux, 4)
        + 2.0 * window(minus_flux, 5)
    ) / 60.0
    face_sum = upwind + downwind
    return lax.slice_in_dim(
        face_sum, stride, (cells + 1) * stride, axis=axis_at
    ) - lax.slice_in_dim(face_sum, 0, cells * stride, axis=axis_at)


def stretch(index_rows, total_rows):
    growth = jnp.exp(STRETCH_RATE * (index_rows + 0.5) / total_rows)
    denominator = math.exp(STRETCH_RATE) - 1.0
    return ((growth - 1.0) / denominator, STRETCH_RATE * growth / (total_rows * denominator))


def split_pair(fluxes, speeds, conserved):
    return (0.5 * (fluxes + speeds * conserved), 0.5 * (fluxes - speeds * conserved))


def stream_part(conserved_x, height_ext, spacing_rows, planes):
    columns = conserved_x.shape[1] - 6
    specific_volume_inverse, vel_x, vel_y, vel_z, thermodynamic_stress, sound_speed = primitives(
        conserved_x
    )
    metric = (
        SPAN_STEP
        * jnp.tile(height_ext, (1, conserved_x.shape[2] // planes))
        * spacing_rows[None, :]
    )
    fluxes = (
        jnp.stack(
            [
                conserved_x[1],
                conserved_x[1] * vel_x + thermodynamic_stress,
                conserved_x[2] * vel_x,
                conserved_x[3] * vel_x,
                (conserved_x[4] + thermodynamic_stress) * vel_x,
                conserved_x[5] * vel_x,
            ]
        )
        * metric
    )
    speeds = (jnp.abs(vel_x) + sound_speed) * metric
    plus_flux, minus_flux = split_pair(fluxes, speeds, conserved_x)
    return face_difference(plus_flux, minus_flux, columns, 1, 1)


def normal_part(conserved_y, slope_x, slope_z, shock_rate, eta_rows, planes):
    copies = conserved_y.shape[2] // planes
    row_count = copies - 6
    specific_volume_inverse, vel_x, vel_y, vel_z, thermodynamic_stress, sound_speed = primitives(
        conserved_y
    )
    face_area = STREAM_STEP * SPAN_STEP
    metric_x = -face_area * eta_rows[None, :] * jnp.tile(slope_x, (1, copies))
    metric_z = -face_area * eta_rows[None, :] * jnp.tile(slope_z, (1, copies))
    metric_t = -face_area * eta_rows[None, :] * jnp.tile(shock_rate, (1, copies))
    contra = metric_t + metric_x * vel_x + face_area * vel_y + metric_z * vel_z
    fluxes = jnp.stack(
        [
            conserved_y[0] * contra,
            conserved_y[1] * contra + metric_x * thermodynamic_stress,
            conserved_y[2] * contra + face_area * thermodynamic_stress,
            conserved_y[3] * contra + metric_z * thermodynamic_stress,
            (conserved_y[4] + thermodynamic_stress) * contra - metric_t * thermodynamic_stress,
            conserved_y[5] * contra,
        ]
    )
    speeds = jnp.abs(contra) + sound_speed * jnp.sqrt(
        metric_x * metric_x + face_area * face_area + metric_z * metric_z
    )
    plus_flux, minus_flux = split_pair(fluxes, speeds, conserved_y)
    return face_difference(plus_flux, minus_flux, row_count, 2, planes)


def span_part(conserved, height, spacing_rows, planes):
    specific_volume_inverse, vel_x, vel_y, vel_z, thermodynamic_stress, sound_speed = primitives(
        conserved
    )
    metric = (
        STREAM_STEP * jnp.tile(height, (1, conserved.shape[2] // planes)) * spacing_rows[None, :]
    )
    fluxes = (
        jnp.stack(
            [
                conserved[3],
                conserved[1] * vel_z,
                conserved[2] * vel_z,
                conserved[3] * vel_z + thermodynamic_stress,
                (conserved[4] + thermodynamic_stress) * vel_z,
                conserved[5] * vel_z,
            ]
        )
        * metric
    )
    speeds = (jnp.abs(vel_z) + sound_speed) * metric
    plus_flux, minus_flux = split_pair(fluxes, speeds, conserved)
    upwind = (
        2.0 * zshift(plus_flux, 2, planes)
        - 13.0 * zshift(plus_flux, 1, planes)
        + 47.0 * plus_flux
        + 27.0 * zshift(plus_flux, -1, planes)
        - 3.0 * zshift(plus_flux, -2, planes)
    ) / 60.0
    downwind = (
        -3.0 * zshift(minus_flux, 1, planes)
        + 27.0 * minus_flux
        + 47.0 * zshift(minus_flux, -1, planes)
        - 13.0 * zshift(minus_flux, -2, planes)
        + 2.0 * zshift(minus_flux, -3, planes)
    ) / 60.0
    face_sum = upwind + downwind
    return face_sum - zshift(face_sum, 1, planes)


def relaxation(conserved):
    specific_volume_inverse, vel_x, vel_y, vel_z, thermodynamic_stress, sound_speed = primitives(
        conserved
    )
    heavy_particle_kelvin = thermodynamic_stress / specific_volume_inverse
    oscillator_balanced_share = CHARACTER_KELVIN / (
        jnp.exp(CHARACTER_KELVIN / heavy_particle_kelvin) - 1.0
    )
    landau_teller_source = thermodynamic_stress / (
        LANDAU_TELLER * jnp.exp(WHITE_LAW_FACTOR * jnp.exp(-jnp.log(heavy_particle_kelvin) / 3.0))
    )
    return (
        specific_volume_inverse
        * (oscillator_balanced_share - conserved[5] / specific_volume_inverse)
        * landau_teller_source
    )


def slopes(height_ext, planes):
    columns = height_ext.shape[0] - 6
    slope_x = (
        height_ext[1 : columns + 1]
        - 8.0 * height_ext[2 : columns + 2]
        + 8.0 * height_ext[4 : columns + 4]
        - height_ext[5 : columns + 5]
    ) / (12.0 * STREAM_STEP)
    height = height_ext[3 : columns + 3]
    slope_z = (
        zshift(height, 2, planes)
        - 8.0 * zshift(height, 1, planes)
        + 8.0 * zshift(height, -1, planes)
        - zshift(height, -2, planes)
    ) / (12.0 * SPAN_STEP)
    return (slope_x, slope_z)


def shock_speed(top_row, slope_x, slope_z):
    specific_volume_inverse, vel_x, vel_y, vel_z, thermodynamic_stress, sound_speed = primitives(
        top_row
    )
    tilt_norm = jnp.sqrt(1.0 + slope_x * slope_x + slope_z * slope_z)
    normal = (vel_y - vel_x * slope_x - vel_z * slope_z) / tilt_norm
    sine_sq = slope_x * slope_x / (tilt_norm * tilt_norm)
    jump_pressure = FREE_PRESSURE * (
        1.0 + 2.0 * HEAT_RATIO / (HEAT_RATIO + 1.0) * (FREE_MACH * FREE_MACH * sine_sq - 1.0)
    )
    return tilt_norm * (
        normal + (jump_pressure - thermodynamic_stress) / (specific_volume_inverse * sound_speed)
    )


def wall_ghosts(first_rows, blowing, planes):
    mirror = jnp.concatenate(
        [
            first_rows[..., 2 * planes : 3 * planes],
            first_rows[..., planes : 2 * planes],
            first_rows[..., 0:planes],
        ],
        axis=-1,
    )
    blown_y = 2.0 * jnp.tile(blowing, (1, 3)) - mirror[2]
    stagnation_enthalpy_sum = (
        mirror[4] + 0.5 * (blown_y * blown_y - mirror[2] * mirror[2]) / mirror[0]
    )
    return jnp.stack([mirror[0], mirror[1], blown_y, mirror[3], stagnation_enthalpy_sum, mirror[5]])


def advance(
    conserved,
    conserved_x,
    conserved_y,
    height_ext,
    slope_x,
    slope_z,
    shock_rate,
    first_row,
    total_rows,
    planes,
):
    columns = conserved.shape[1]
    row_count = conserved.shape[2] // planes
    local_rows = (first_row + jnp.arange(row_count, dtype=jnp.int32)).astype(jnp.float32)
    eta_local, spacing_local = stretch(local_rows, total_rows)
    spacing_rows = jnp.repeat(spacing_local, planes)
    outer_rows = (first_row - 3 + jnp.arange(row_count + 6, dtype=jnp.int32)).astype(jnp.float32)
    eta_outer = stretch(outer_rows, total_rows)[0]
    eta_rows = jnp.repeat(eta_outer, planes)
    height = height_ext[3 : columns + 3]
    divergence = (
        stream_part(conserved_x, height_ext, spacing_rows, planes)
        + normal_part(conserved_y, slope_x, slope_z, shock_rate, eta_rows, planes)
        + span_part(conserved, height, spacing_rows, planes)
    )
    height_rows = jnp.tile(height, (1, row_count))
    rate_rows = jnp.tile(shock_rate, (1, row_count))
    volume = STREAM_STEP * SPAN_STEP * height_rows * spacing_rows[None, :]
    change = -divergence / volume - conserved * (rate_rows / height_rows)
    change = jnp.concatenate([change[:5], (change[5] + relaxation(conserved))[None]], axis=0)
    return conserved + COURANT / total_rows * change


def edge_fill(values, axis_at, cells, device_at, devices):
    positions = jnp.arange(cells + 6, dtype=jnp.int32)
    processor_arrangement = [1] * values.ndim
    processor_arrangement[axis_at] = cells + 6
    positions = positions.reshape(processor_arrangement)
    leading = lax.slice_in_dim(values, 3, 4, axis=axis_at)
    trailing = lax.slice_in_dim(values, cells + 2, cells + 3, axis=axis_at)
    values = jnp.where((device_at == 0) & (positions < 3), leading, values)
    return jnp.where((device_at == devices - 1) & (positions >= cells + 3), trailing, values)


def wall_flux(wall_segment, segment_level, blow_table):
    seg_hit = wall_segment[:, None] == jnp.arange(segment_level.shape[0], dtype=jnp.int32)[None, :]
    levels = jnp.sum(jnp.where(seg_hit, segment_level[None, :], 0), axis=1)
    level_hit = levels[:, None] == jnp.arange(blow_table.shape[0], dtype=jnp.int32)[None, :]
    return jnp.sum(jnp.where(level_hit[:, :, None], blow_table[None, :, :], 0.0), axis=1)


def shards(state, shock_height, wall_segment, segment_level, blow_table):
    planes = blow_table.shape[1]
    columns = state.shape[1]
    length = state.shape[2]
    row_count = length // planes
    col_devs = lax.axis_size("gx")
    row_devs = lax.axis_size("gy")
    col_dev = lax.axis_index("gx")
    row_dev = lax.axis_index("gy")
    total_rows = row_count * row_devs
    conserved_x = padded(state, (("gx", 1),), 3)
    height_ext = padded(shock_height, (("gx", 0),), 3)
    conserved_x = edge_fill(conserved_x, 1, columns, col_dev, col_devs)
    height_ext = edge_fill(height_ext, 0, columns, col_dev, col_devs)
    slope_x, slope_z = slopes(height_ext, planes)
    own_rate = shock_speed(state[:, :, length - planes :], slope_x, slope_z)
    shock_rate = broadcast(own_rate, "gy", row_devs - 1)
    blowing = wall_flux(wall_segment, segment_level, blow_table)
    halo_y = padded(state, (("gy", 2),), 3 * planes)
    ghost_below = jnp.where(
        row_dev == 0,
        wall_ghosts(state[..., : 3 * planes], blowing, planes),
        halo_y[..., : 3 * planes],
    )
    ghost_above = jnp.where(
        row_dev == row_devs - 1,
        jnp.tile(state[..., length - planes :], (1, 1, 3)),
        halo_y[..., length + 3 * planes :],
    )
    conserved_y = jnp.concatenate([ghost_below, state, ghost_above], axis=2)
    state_new = advance(
        state,
        conserved_x,
        conserved_y,
        height_ext,
        slope_x,
        slope_z,
        shock_rate,
        row_dev * row_count,
        total_rows,
        planes,
    )
    shock_new = shock_height + COURANT / total_rows * shock_rate
    return (state_new, shock_new)


def solution(mesh):
    in_specs = (P(None, "gx", "gy"), P("gx", None), P("gx"), P(), P())
    out_specs = (P(None, "gx", "gy"), P("gx", None))
    return jax.shard_map(shards, mesh=mesh, in_specs=in_specs, out_specs=out_specs, check_vma=False)
```

profile of v0, /device:TPU:9, one launch (start us, length us, event | category | flops | bytes accessed | tf_op | source)
XLA Modules:
  0.0 97.4 jit_solution(18221725842695820436)
XLA Ops:
  1.5 3.1 %collective-permute-start.2 = (f32[3,32]{1,0:T(4,128)S(1)}, f32[3,32]{1,0:T(4,128)S(1)}, u32[]{:S(2)}, u32[]{:S(2)}) collective-permute-start(f32[3,32]{1,0:T(4,128)S(1)} %get-tuple-element.71), channel_id=1, source_target_pairs={{0,2},{2,4},{4,6},{6,8},{8,10},{10,12},{12,14},{14,16},{16,18},{18... | collective-permute-start | bytes 1160 | tf_op jit(solution)/shard_map/ppermute | solution.py:25
  4.6 4.0 %collective-permute-start.3 = (f32[3,32]{1,0:T(4,128)S(1)}, f32[3,32]{1,0:T(4,128)S(1)}, u32[]{:S(2)}, u32[]{:S(2)}) collective-permute-start(f32[3,32]{1,0:T(4,128)S(1)} %get-tuple-element.72), channel_id=1, source_target_pairs={{2,0},{4,2},{6,4},{8,6},{10,8},{12,10},{14,12},{16,14},{18,16},{20... | collective-permute-start | bytes 1160 | tf_op jit(solution)/shard_map/ppermute | solution.py:28
  8.5 2.2 %fusion.97 = (f32[6,3,3072]{2,1,0:T(4,128)}, f32[6,3,3072]{2,1,0:T(4,128)}) fusion(f32[6,16,3072]{2,1,0:T(8,128)} %param.5), kind=kLoop, calls=%fused_computation.217 | loop fusion | bytes 884736 | tf_op jit(solution)/shard_map/slice | solution.py:26
  10.7 1.9 %collective-permute-start = (f32[6,3,3072]{2,1,0:T(4,128)}, f32[6,3,3072]{2,1,0:T(4,128)}, u32[]{:S(2)}, u32[]{:S(2)}) collective-permute-start(f32[6,3,3072]{2,1,0:T(4,128)} %get-tuple-element.50), channel_id=1, source_target_pairs={{0,2},{2,4},{4,6},{6,8},{8,10},{10,12},{12,14},{14,16},{16,18},{18... | collective-permute-start | bytes 663560 | tf_op jit(solution)/shard_map/ppermute | solution.py:25
  12.6 5.2 %collective-permute-start.1 = (f32[6,3,3072]{2,1,0:T(4,128)}, f32[6,3,3072]{2,1,0:T(4,128)}, u32[]{:S(2)}, u32[]{:S(2)}) collective-permute-start(f32[6,3,3072]{2,1,0:T(4,128)} %get-tuple-element.51), channel_id=1, source_target_pairs={{2,0},{4,2},{6,4},{8,6},{10,8},{12,10},{14,12},{16,14},{18,16},{20... | collective-permute-start | bytes 663560 | tf_op jit(solution)/shard_map/ppermute | solution.py:28
  18.5 1.3 %collective-permute-start.4 = (f32[6,16,96]{2,1,0:T(8,128)}, f32[6,16,96]{2,1,0:T(8,128)}, u32[]{:S(2)}, u32[]{:S(2)}) collective-permute-start(f32[6,16,96]{2,1,0:T(8,128)} %get-tuple-element.53), channel_id=1, source_target_pairs={{0,1},{2,3},{4,5},{6,7},{8,9},{10,11},{12,13},{14,15},{16,17},{18,... | collective-permute-start | bytes 110600 | tf_op jit(solution)/shard_map/ppermute | solution.py:25
  27.0 4.9 %collective-permute-start.5 = (f32[6,16,96]{2,1,0:T(8,128)}, f32[6,16,96]{2,1,0:T(8,128)}, u32[]{:S(2)}, u32[]{:S(2)}) collective-permute-start(f32[6,16,96]{2,1,0:T(8,128)} %get-tuple-element.52), channel_id=1, source_target_pairs={{1,0},{3,2},{5,4},{7,6},{9,8},{11,10},{13,12},{15,14},{17,16},{19,... | collective-permute-start | bytes 110600 | tf_op jit(solution)/shard_map/ppermute | solution.py:28
  34.7 1.1 %tile.92 = f32[16,3072]{1,0:T(8,128)} reshape(f32[16,96,32]{2,1,0:T(8,128)S(1)} %tile.91) | data formatting | bytes 393216 | tf_op jit(solution)/shard_map/tile | solution.py:166
  35.8 1.0 %tile.93 = f32[1,16,3072]{2,1,0:T(8,128)} reshape(f32[16,96,32]{2,1,0:T(8,128)S(1)} %tile.91) | data formatting | bytes 393216 | tf_op jit(solution)/shard_map/tile | solution.py:166
  36.8 1.5 %fusion.79 = (f32[16,32]{1,0:T(8,128)S(1)}, f32[16,32]{1,0:T(8,128)}, f32[16,32]{1,0:T(8,128)}) fusion(f32[6,16,3072]{2,1,0:T(8,128)S(1)} %copy-done, pred[]{:T(512)S(6)} %eq.69, f32[22,32]{1,0:T(8,128)S(1)} %fusion.56, f32[16,2]{1,0:T(8,128)} %get-tuple-element.62, f32[16,30]{1,0:T(8,128)} %get-tuple-element.64, f32[16,1]{1,0:T(8,128)} %get-tuple-element.66, ...), kind=kLoop, calls=%fused_computation.193 | loop fusion | flops 26624 | bytes 34817 | tf_op jit(solution)/shard_map/jit(_where)/select_n | solution.py:35
  38.3 3.1 %psum.7 = f32[16,32]{1,0:T(8,128)} all-reduce(f32[16,32]{1,0:T(8,128)S(1)} %get-tuple-element.12), channel_id=1, replica_groups=mesh['gx'=16,'gy'=2] {'gy'}, use_global_device_ids=true, to_apply=%region_2.3 | all-reduce | flops 512 | bytes 4096 | tf_op jit(solution)/shard_map/psum | solution.py:35
  42.1 1.1 %tile.95 = f32[16,3072]{1,0:T(8,128)} reshape(f32[16,96,32]{2,1,0:T(8,128)S(1)} %tile.94) | data formatting | bytes 393216 | tf_op jit(solution)/shard_map/tile | solution.py:295
  43.2 1.1 %multiply_dynamic-update-slice_fusion.7 = (f32[6,16,3072]{2,1,0:T(8,128)S(1)}, f32[16,3072]{1,0:T(8,128)S(1)}) fusion(f32[6,16,3072]{2,1,0:T(8,128)S(1)} %get-tuple-element.2, f32[1,16,3072]{2,1,0:T(8,128)S(1)} %get-tuple-element.5, f32[6,16,3072]{2,1,0:T(8,128)S(1)} %copy-done, f32[1,16,3072]{2,1,0:T(8,128)S(1)} %get-tuple-element.3, ...), kind=kLoop, calls=%fused_computation.122 | loop fusion | flops 442368 | bytes 1388544
  46.0 1.8 %fusion.85 = (f32[6,16,3041]{2,1,0:T(8,128)}, f32[6,16,3041]{2,1,0:T(8,128)}) fusion(f32[6,16,3072]{2,1,0:T(8,128)S(1)} %get-tuple-element.19), kind=kLoop, calls=%fused_computation.205 | loop fusion | bytes 4670976 | tf_op jit(solution)/shard_map/jit(_roll_static)/slice | solution.py:50
  47.7 1.8 %fusion.86 = (f32[6,16,3071]{2,1,0:T(8,128)}, f32[6,16,3071]{2,1,0:T(8,128)}) fusion(f32[6,16,3072]{2,1,0:T(8,128)S(1)} %get-tuple-element.19), kind=kLoop, calls=%fused_computation.206 | loop fusion | bytes 4717056 | tf_op jit(solution)/shard_map/jit(_roll_static)/slice | solution.py:49
  49.6 1.8 %fusion.89 = (f32[6,16,3042]{2,1,0:T(8,128)}, f32[6,16,3042]{2,1,0:T(8,128)}) fusion(f32[6,16,3072]{2,1,0:T(8,128)S(1)} %get-tuple-element.20), kind=kLoop, calls=%fused_computation.209 | loop fusion | bytes 4672512 | tf_op jit(solution)/shard_map/jit(_roll_static)/slice | solution.py:50
  51.4 1.8 %fusion.90 = (f32[6,16,3070]{2,1,0:T(8,128)}, f32[6,16,3070]{2,1,0:T(8,128)}) fusion(f32[6,16,3072]{2,1,0:T(8,128)S(1)} %get-tuple-element.20), kind=kLoop, calls=%fused_computation.210 | loop fusion | bytes 4715520 | tf_op jit(solution)/shard_map/jit(_roll_static)/slice | solution.py:49
  53.2 1.9 %fusion.93 = (f32[6,16,3041]{2,1,0:T(8,128)}, f32[6,16,3041]{2,1,0:T(8,128)}) fusion(f32[6,16,3072]{2,1,0:T(8,128)S(1)} %get-tuple-element.20), kind=kLoop, calls=%fused_computation.213 | loop fusion | bytes 4670976 | tf_op jit(solution)/shard_map/jit(_roll_static)/slice | solution.py:50
  55.0 1.8 %fusion.94 = (f32[6,16,3071]{2,1,0:T(8,128)}, f32[6,16,3071]{2,1,0:T(8,128)}) fusion(f32[6,16,3072]{2,1,0:T(8,128)S(1)} %get-tuple-element.20), kind=kLoop, calls=%fused_computation.214 | loop fusion | bytes 4717056 | tf_op jit(solution)/shard_map/jit(_roll_static)/slice | solution.py:49
  56.8 1.4 %slice.663 = f32[6,16,3070]{2,1,0:T(8,128)} slice(f32[6,16,3072]{2,1,0:T(8,128)S(1)} %get-tuple-element.19), slice={[0:6], [0:16], [2:3072]} | slice | bytes 2357760 | tf_op jit(solution)/shard_map/jit(_roll_static)/slice | solution.py:49
  58.2 1.4 %slice.667 = f32[6,16,3069]{2,1,0:T(8,128)} slice(f32[6,16,3072]{2,1,0:T(8,128)S(1)} %get-tuple-element.19), slice={[0:6], [0:16], [3:3072]} | slice | bytes 2356992 | tf_op jit(solution)/shard_map/jit(_roll_static)/slice | solution.py:49
  65.9 1.2 %tile.35 = f32[22,3072]{1,0:T(8,128)} reshape(f32[22,96,32]{2,1,0:T(8,128)S(1)} %tile.34) | data formatting | bytes 540672 | tf_op jit(solution)/shard_map/tile | solution.py:112
  67.2 1.7 %broadcast_multiply_fusion.2 = f32[22,3072]{1,0:T(8,128)} fusion(f32[22,3072]{1,0:T(8,128)} %tile.35, f32[3072]{0:T(1024)S(1)} %copy-done.18), kind=kLoop, calls=%fused_computation.132 | loop fusion | flops 67584 | bytes 552960 | tf_op jit(solution)/shard_map/mul | solution.py:111
  68.9 8.5 %fusion.32 = f32[6,16,3072]{2,1,0:T(8,128)S(1)} fusion(f32[6,16,3070]{2,1,0:T(8,128)} %get-tuple-element.37, f32[6,16,2]{2,1,0:T(8,128)} %get-tuple-element.39, f32[6,16,30]{2,1,0:T(8,128)} %get-tuple-element.33, f32[6,16,3042]{2,1,0:T(8,128)} %get-tuple-element.35, f32[6,16,3071]{2,1,0:T(8,128)} %get-tuple-element.45, f32[6,16,1]{2,1,0:T(8,128)} %get-tuple-element.47, ...), kind=kLoop, calls=%fused_computation.60 | loop fusion | flops 14155776 | bytes 22821888 | tf_op jit(solution)/shard_map/add | solution.py:197
  78.1 1.4 %slice.673 = f32[6,16,3041]{2,1,0:T(8,128)} slice(f32[6,16,3072]{2,1,0:T(8,128)S(1)} %fusion.32), slice={[0:6], [0:16], [31:3072]} | slice | bytes 2335488 | tf_op jit(solution)/shard_map/jit(_roll_static)/slice | solution.py:45
  82.0 1.4 %broadcast_select_fusion.1 = f32[6,16,96]{2,1,0:T(8,128)} fusion(f32[6,16,96]{2,1,0:T(8,128)S(1)} %copy-done.23, f32[6,16,96]{2,1,0:T(8,128)} %collective-permute-done.4, pred[]{:T(512)S(6)} %eq.62), kind=kLoop, calls=%fused_computation.145 | loop fusion | flops 9216 | bytes 110593 | tf_op jit(solution)/shard_map/jit(_where)/select_n | solution.py:339
  83.4 1.7 %concatenate.126 = f32[6,16,3264]{2,1,0:T(8,128)S(1)} concatenate(f32[6,16,96]{2,1,0:T(8,128)} %broadcast_select_fusion.1, f32[6,16,3072]{2,1,0:T(8,128)S(1)} %copy-done, f32[6,16,96]{2,1,0:T(8,128)S(1)} %broadcast_select_fusion), dimensions={2} | concatenate | bytes 2506752 | tf_op jit(solution)/shard_map/concatenate | solution.py:349
  86.1 2.3 %fusion.13 = f32[6,16,3104]{2,1,0:T(8,128)S(1)} fusion(f32[6,16,3264]{2,1,0:T(8,128)S(1)} %get-tuple-element.18, f32[6,16,3264]{2,1,0:T(8,128)S(1)} %get-tuple-element.17), kind=kLoop, calls=%fused_computation.29 | loop fusion | flops 5959680 | bytes 13111296 | tf_op jit(solution)/shard_map/add | solution.py:89
  88.4 1.4 %fusion.10 = f32[6,22,3072]{2,1,0:T(8,128)S(1)} fusion(f32[6,3,3072]{2,1,0:T(4,128)} %collective-permute-done.1, f32[6,16,3072]{2,1,0:T(8,128)S(1)} %copy-done, f32[6,3,3072]{2,1,0:T(4,128)} %collective-permute-done, f32[6,3072]{1,0:T(8,128)S(1)} %copy-done.15, f32[6,3072]{1,0:T(8,128)S(1)} %copy-done.16, pred[22]{0:T(512)(128)(4,1)S(1)} %copy-done.37, ...), kind=kLoop, calls=%fused_computation.21 | loop fusion | flops 1622016 | bytes 3391532 | tf_op jit(solution)/shard_map/jit(_where)/select_n | solution.py:310
  91.8 2.2 %fusion.2 = f32[6,17,3072]{2,1,0:T(8,128)S(1)} fusion(f32[6,22,3072]{2,1,0:T(8,128)S(1)} %get-tuple-element.16, f32[6,22,3072]{2,1,0:T(8,128)S(1)} %get-tuple-element.15), kind=kLoop, calls=%fused_computation.3 | loop fusion | flops 6266880 | bytes 13787136 | tf_op jit(solution)/shard_map/add | solution.py:89
  94.1 0.9 fusion.25
  96.2 1.2 %fusion.45 = f32[6,16,3072]{2,1,0:T(8,128)} fusion(f32[6,16,3072]{2,1,0:T(8,128)S(1)} %copy-done, f32[1,16,3072]{2,1,0:T(8,128)S(1)} %slice_add_fusion, f32[5,16,3072]{2,1,0:T(8,128)S(1)} %slice.675), kind=kLoop, calls=%fused_computation.82 | loop fusion | flops 884736 | bytes 3538944 | tf_op jit(solution)/shard_map/add | solution.py:299
  (176 shorter events, 26.8 us)
Async XLA Ops:
  0.6 19.2 %copy-start.24 = (f32[16,32]{1,0:T(8,128)S(1)}, f32[16,32]{1,0:T(8,128)}, u32[]{:S(2)}) copy-start(f32[16,32]{1,0:T(8,128)} %param.6) | copy-start | bytes 6148
  0.6 17.2 %copy-start = (f32[6,16,3072]{2,1,0:T(8,128)S(1)}, f32[6,16,3072]{2,1,0:T(8,128)}, u32[]{:S(2)}) copy-start(f32[6,16,3072]{2,1,0:T(8,128)} %param.5) | copy-start | bytes 3538948
  1.5 25.5 %collective-permute-start.2 = (f32[3,32]{1,0:T(4,128)S(1)}, f32[3,32]{1,0:T(4,128)S(1)}, u32[]{:S(2)}, u32[]{:S(2)}) collective-permute-start(f32[3,32]{1,0:T(4,128)S(1)} %get-tuple-element.71), channel_id=1, source_target_pairs={{0,2},{2,4},{4,6},{6,8},{8,10},{10,12},{12,14},{14,16},{16,18},{18... | collective-permute-start | bytes 1160 | tf_op jit(solution)/shard_map/ppermute | solution.py:25
  4.6 27.3 %collective-permute-start.3 = (f32[3,32]{1,0:T(4,128)S(1)}, f32[3,32]{1,0:T(4,128)S(1)}, u32[]{:S(2)}, u32[]{:S(2)}) collective-permute-start(f32[3,32]{1,0:T(4,128)S(1)} %get-tuple-element.72), channel_id=1, source_target_pairs={{2,0},{4,2},{6,4},{8,6},{10,8},{12,10},{14,12},{16,14},{18,16},{20... | collective-permute-start | bytes 1160 | tf_op jit(solution)/shard_map/ppermute | solution.py:28
  10.7 77.6 %collective-permute-start = (f32[6,3,3072]{2,1,0:T(4,128)}, f32[6,3,3072]{2,1,0:T(4,128)}, u32[]{:S(2)}, u32[]{:S(2)}) collective-permute-start(f32[6,3,3072]{2,1,0:T(4,128)} %get-tuple-element.50), channel_id=1, source_target_pairs={{0,2},{2,4},{4,6},{6,8},{8,10},{10,12},{12,14},{14,16},{16,18},{18... | collective-permute-start | bytes 663560 | tf_op jit(solution)/shard_map/ppermute | solution.py:25
  12.6 75.7 %collective-permute-start.1 = (f32[6,3,3072]{2,1,0:T(4,128)}, f32[6,3,3072]{2,1,0:T(4,128)}, u32[]{:S(2)}, u32[]{:S(2)}) collective-permute-start(f32[6,3,3072]{2,1,0:T(4,128)} %get-tuple-element.51), channel_id=1, source_target_pairs={{2,0},{4,2},{6,4},{8,6},{10,8},{12,10},{14,12},{16,14},{18,16},{20... | collective-permute-start | bytes 663560 | tf_op jit(solution)/shard_map/ppermute | solution.py:28
  18.5 63.4 %collective-permute-start.4 = (f32[6,16,96]{2,1,0:T(8,128)}, f32[6,16,96]{2,1,0:T(8,128)}, u32[]{:S(2)}, u32[]{:S(2)}) collective-permute-start(f32[6,16,96]{2,1,0:T(8,128)} %get-tuple-element.53), channel_id=1, source_target_pairs={{0,1},{2,3},{4,5},{6,7},{8,9},{10,11},{12,13},{14,15},{16,17},{18,... | collective-permute-start | bytes 110600 | tf_op jit(solution)/shard_map/ppermute | solution.py:25
  20.5 48.4 %copy-start.29 = (pred[3072]{0:T(1024)(128)(4,1)}, pred[3072]{0:T(1024)(128)(4,1)S(1)}, u32[]{:S(2)}) copy-start(pred[3072]{0:T(1024)(128)(4,1)S(1)} %get-tuple-element.82) | copy-start | bytes 9220
  22.9 20.3 %copy-start.7 = (f32[1,16,3072]{2,1,0:T(8,128)}, f32[1,16,3072]{2,1,0:T(8,128)S(1)}, u32[]{:S(2)}) copy-start(f32[1,16,3072]{2,1,0:T(8,128)S(1)} %get-tuple-element.3) | copy-start | bytes 589828
  23.9 10.7 %copy-start.22 = (f32[6,16,96]{2,1,0:T(8,128)}, f32[6,16,96]{2,1,0:T(8,128)S(1)}, u32[]{:S(2)}) copy-start(f32[6,16,96]{2,1,0:T(8,128)S(1)} %constant_dynamic-update-slice_fusion) | copy-start | bytes 110596
  23.9 10.7 %copy-start.36 = (pred[22]{0:T(512)(128)(4,1)}, pred[22]{0:T(512)(128)(4,1)S(1)}, u32[]{:S(2)}) copy-start(pred[22]{0:T(512)(128)(4,1)S(1)} %get-tuple-element.73) | copy-start | bytes 70
  23.9 10.7 %copy-start.38 = (pred[22]{0:T(512)(128)(4,1)}, pred[22]{0:T(512)(128)(4,1)S(1)}, u32[]{:S(2)}) copy-start(pred[22]{0:T(512)(128)(4,1)S(1)} %get-tuple-element.74) | copy-start | bytes 70
  27.0 54.5 %collective-permute-start.5 = (f32[6,16,96]{2,1,0:T(8,128)}, f32[6,16,96]{2,1,0:T(8,128)}, u32[]{:S(2)}, u32[]{:S(2)}) collective-permute-start(f32[6,16,96]{2,1,0:T(8,128)} %get-tuple-element.52), channel_id=1, source_target_pairs={{1,0},{3,2},{5,4},{7,6},{9,8},{11,10},{13,12},{15,14},{17,16},{19,... | collective-permute-start | bytes 110600 | tf_op jit(solution)/shard_map/ppermute | solution.py:28
  65.8 1.3 %copy-start.18 = (f32[3072]{0:T(1024)S(1)}, f32[3072]{0:T(1024)}, u32[]{:S(2)}) copy-start(f32[3072]{0:T(1024)} %mul.794) | copy-start | bytes 36868
  65.9 3.0 %copy-start.31 = (pred[3072]{0:T(1024)(128)(4,1)S(1)}, pred[3072]{0:T(1024)(128)(4,1)}, u32[]{:S(2)}) copy-start(pred[3072]{0:T(1024)(128)(4,1)} %get-tuple-element.81) | copy-start | bytes 9220
  65.9 3.0 %copy-start.32 = (pred[3072]{0:T(1024)(128)(4,1)S(1)}, pred[3072]{0:T(1024)(128)(4,1)}, u32[]{:S(2)}) copy-start(pred[3072]{0:T(1024)(128)(4,1)} %get-tuple-element.79) | copy-start | bytes 9220
  65.9 2.9 %copy-start.33 = (pred[3072]{0:T(1024)(128)(4,1)S(1)}, pred[3072]{0:T(1024)(128)(4,1)}, u32[]{:S(2)}) copy-start(pred[3072]{0:T(1024)(128)(4,1)} %get-tuple-element.80) | copy-start | bytes 9220
  65.9 2.9 %copy-start.34 = (pred[3072]{0:T(1024)(128)(4,1)S(1)}, pred[3072]{0:T(1024)(128)(4,1)}, u32[]{:S(2)}) copy-start(pred[3072]{0:T(1024)(128)(4,1)} %fusion.63) | copy-start | bytes 9220
  68.9 8.6 %copy-start.21 = (f32[16,32]{1,0:T(8,128)S(1)}, f32[16,32]{1,0:T(8,128)}, u32[]{:S(2)}) copy-start(f32[16,32]{1,0:T(8,128)} %psum.7) | copy-start | bytes 6148
  68.9 8.6 %copy-start.25 = (f32[16,32]{1,0:T(8,128)S(1)}, f32[16,32]{1,0:T(8,128)}, u32[]{:S(2)}) copy-start(f32[16,32]{1,0:T(8,128)} %param.6) | copy-start | bytes 6148
  77.5 2.1 %copy-start.1 = (f32[6,16,3072]{2,1,0:T(8,128)}, f32[6,16,3072]{2,1,0:T(8,128)S(1)}, u32[]{:S(2)}) copy-start(f32[6,16,3072]{2,1,0:T(8,128)S(1)} %fusion.32) | copy-start | bytes 3538948
  83.4 1.7 %copy-start.14 = (f32[3264]{0:T(1024)S(1)}, f32[3264]{0:T(1024)}, u32[]{:S(2)}) copy-start(f32[3264]{0:T(1024)} %mul.830) | copy-start | bytes 39172
  86.0 2.3 %copy-start.15 = (f32[6,3072]{1,0:T(8,128)S(1)}, f32[6,3072]{1,0:T(8,128)}, u32[]{:S(2)}) copy-start(f32[6,3072]{1,0:T(8,128)} %get-tuple-element.77) | copy-start | bytes 221188
  86.0 2.3 %copy-start.16 = (f32[6,3072]{1,0:T(8,128)S(1)}, f32[6,3072]{1,0:T(8,128)}, u32[]{:S(2)}) copy-start(f32[6,3072]{1,0:T(8,128)} %get-tuple-element.78) | copy-start | bytes 221188
  86.0 2.3 %copy-start.37 = (pred[22]{0:T(512)(128)(4,1)S(1)}, pred[22]{0:T(512)(128)(4,1)}, u32[]{:S(2)}) copy-start(pred[22]{0:T(512)(128)(4,1)} %copy-done.36) | copy-start | bytes 70
  86.1 2.3 %copy-start.39 = (pred[22]{0:T(512)(128)(4,1)S(1)}, pred[22]{0:T(512)(128)(4,1)}, u32[]{:S(2)}) copy-start(pred[22]{0:T(512)(128)(4,1)} %copy-done.38) | copy-start | bytes 70
  88.4 1.5 %copy-start.19 = (f32[3072]{0:T(1024)S(1)}, f32[3072]{0:T(1024)}, u32[]{:S(2)}) copy-start(f32[3072]{0:T(1024)} %mul.794) | copy-start | bytes 36868
  91.8 2.3 %copy-start.2 = (f32[6,16,3072]{2,1,0:T(8,128)S(1)}, f32[6,16,3072]{2,1,0:T(8,128)}, u32[]{:S(2)}) copy-start(f32[6,16,3072]{2,1,0:T(8,128)} %copy-done.1) | copy-start | bytes 3538948
  91.8 2.3 %copy-start.4 = (f32[6,16,3041]{2,1,0:T(8,128)S(1)}, f32[6,16,3041]{2,1,0:T(8,128)}, u32[]{:S(2)}) copy-start(f32[6,16,3041]{2,1,0:T(8,128)} %slice.673) | copy-start | bytes 3503236
  91.8 2.3 %copy-start.12 = (f32[16,3072]{1,0:T(8,128)S(1)}, f32[16,3072]{1,0:T(8,128)}, u32[]{:S(2)}) copy-start(f32[16,3072]{1,0:T(8,128)} %get-tuple-element.58) | copy-start | bytes 589828
  91.8 2.3 %copy-start.13 = (f32[16,3072]{1,0:T(8,128)S(1)}, f32[16,3072]{1,0:T(8,128)}, u32[]{:S(2)}) copy-start(f32[16,3072]{1,0:T(8,128)} %get-tuple-element.59) | copy-start | bytes 589828
  91.8 2.3 %copy-start.30 = (pred[3072]{0:T(1024)(128)(4,1)S(1)}, pred[3072]{0:T(1024)(128)(4,1)}, u32[]{:S(2)}) copy-start(pred[3072]{0:T(1024)(128)(4,1)} %copy-done.29) | copy-start | bytes 9220
  (16 other events, 14.9 us)
where the time goes:
time: 98.1 us; the launch traced here: 97.4 us
  local copies, waits for them, and re-layouts  43.7 us (45%)
  other arithmetic  28.7 us (29%)
  starting transfers between devices  20.3 us (21%)
  blocking collectives  3.07 us (3%)
  between operations  1.6 us (2%)
    ppermute x3, starting transfers between devices, padded(): lax.ppermute(lax.slice_in_dim(block, 0, width, axis=dim), axis, backward)  14 us
    slice x15, local copies, waits for them, and re-layouts, zshift(): jnp.roll(values, offset, axis=-1)  13.7 us
    slice x8, local copies, waits for them, and re-layouts, zshift(): jnp.roll(values, offset + planes, axis=-1)  8.92 us
    add x1, other arithmetic, span_part(): face_sum = upwind + downwind  8.53 us
    ppermute x3, starting transfers between devices, padded(): lax.ppermute(lax.slice_in_dim(block, block.shape[dim] - width, None, axis...  6.3 us
    add x2, other arithmetic, face_difference(): face_sum = upwind + downwind  4.5 us
    unnamed x87, local copies, waits for them, and re-layouts  3.51 us
    psum x1, blocking collectives, broadcast(): return lax.psum(jnp.where(mine, array, jnp.zeros_like(array)), axis)  3.07 us
  transfers between devices with their start and end apart: 6, of which 0 were waited for; matrix products, arithmetic and copies ran while one was open for 63% of the time, Pallas kernels for 0%

commit v1 on v0

v1 whole, which is shorter than its diff:
```python
import functools
import math

import jax
import jax.numpy as jnp
import numpy as np
from jax import lax
from jax.experimental import pallas as pl
from jax.experimental.pallas import tpu as pltpu
from jax.sharding import PartitionSpec as P

MESH = pl.DeviceIdType.MESH
COURANT = 0.05
CENTRAL = {-3: -1, -2: 9, -1: -45, 1: 45, 2: -9, 3: 1}
DAMPING = {-3: -1, -2: 6, -1: -15, 0: 20, 1: -15, 2: 6, 3: -1}
DEN = math.exp(2.0) - 1.0
F32 = jnp.float32
BF16 = jnp.bfloat16
PARTS = 3


def stencil_matrices(cols, planes):
    tables = (CENTRAL, DAMPING, CENTRAL, DAMPING)
    rows = 128 // planes
    mx = np.zeros((6, cols, 4, 6, cols), np.float32)
    mz = np.zeros((4, 128, 128), np.float32)
    my = np.zeros((3, 4, 128, 128), np.float32)
    groups = 24 // PARTS
    mh = np.zeros((groups, cols, 2, 4, groups, 3), np.float32)
    for s, table in enumerate(tables):
        for d, coef in table.items():
            for i in range(cols):
                k = i + d
                if 0 <= k < cols:
                    for v in range(6):
                        mx[v, i, s, v, k] = coef
                elif k < 0:
                    for g in range(groups):
                        mh[g, i, 0, s, g, k + 3] = coef
                else:
                    for g in range(groups):
                        mh[g, i, 1, s, g, k - cols] = coef
            for lane in range(128):
                b, z = divmod(lane, planes)
                mz[s, b * planes + (z + d) % planes, lane] += coef
                delta, src = divmod(b + d, rows)
                my[delta + 1, s, src * planes + z, lane] += coef
    return (
        mx.reshape(6 * cols, 24 * cols),
        mz.reshape(512, 128),
        my.reshape(3, 512, 128),
        mh.reshape(groups * cols, 24 * groups),
    )


def primitives(q):
    r = 1.0 / q[0]
    u, v, w = q[1] * r, q[2] * r, q[3] * r
    p = 0.4 * (q[4] - 0.5 * (q[1] * u + q[2] * v + q[3] * w) - q[5])
    c2 = 1.4 * p * r
    return r, u, v, w, p, c2 * lax.rsqrt(c2)


def split(x):
    hi = x.astype(BF16)
    return hi, (x - hi.astype(F32)).astype(BF16)


def kernel(
    n_gx, n_gy, planes,
    q_ref, h_ref, ws_ref, sl_ref, bt_ref, mx_hbm, mz_hbm, my_hbm, mh_hbm,
    out_ref, shock_ref,
    send_lo, send_hi, recv_lo, recv_hi, hx, below, above, top,
    rx, zs, ys, keep, rh, mx, mz, my, mh, blow,
    mat_sem, s_lo, s_hi, r_lo, r_hi, hs_sem, hr_sem, ys_sem, yr_sem, ts_sem, tr_sem,
):
    cols, length = q_ref.shape[1], q_ref.shape[2]
    tiles = length // 128
    per_tile = 128 // planes
    total_rows = n_gy * (length // planes)
    dt = COURANT / total_rows
    ix, iy = lax.axis_index("gx"), lax.axis_index("gy")
    last = tiles * 128 - 128
    groups = tiles // PARTS
    has_l, has_r = ix > 0, ix < n_gx - 1
    has_b, has_a = iy > 0, iy < n_gy - 1
    is_top = iy == n_gy - 1

    mats = [
        pltpu.make_async_copy(a, b, mat_sem.at[i])
        for i, (a, b) in enumerate(((mx_hbm, mx), (mz_hbm, mz), (my_hbm, my), (mh_hbm, mh)))
    ]
    for m in mats:
        m.start()

    barrier = pltpu.get_barrier_semaphore()
    count = has_l.astype(jnp.int32) + has_r.astype(jnp.int32)

    @pl.when(has_l)
    def _():
        pl.semaphore_signal(barrier, inc=1, device_id=(ix - 1, iy), device_id_type=MESH)

    @pl.when(has_r)
    def _():
        pl.semaphore_signal(barrier, inc=1, device_id=(ix + 1, iy), device_id_type=MESH)

    for d in range(n_gy):
        near = (iy - d == 1) | (d - iy == 1) | ((iy != d) & (is_top | (d == n_gy - 1)))
        count = count + near.astype(jnp.int32)

        @pl.when(near)
        def _(d=d):
            pl.semaphore_signal(barrier, inc=1, device_id=(ix, d), device_id_type=MESH)

    for b in range(per_tile):
        hx[8 : 8 + cols, b * planes : (b + 1) * planes] = h_ref[...]

    def lanes(g, k):
        return slice((g * PARTS + k) * 128, (g * PARTS + k) * 128 + 128)

    def pack(k):
        for v in range(6):
            for g in range(groups):
                at = (v * groups + g) * 3
                send_lo[k, at : at + 3, :] = q_ref[v, 0:3, lanes(g, k)]
                send_hi[k, at : at + 3, :] = q_ref[v, cols - 3 : cols, lanes(g, k)]

    def to_left(k):
        return pltpu.make_async_remote_copy(
            send_lo.at[k], recv_hi.at[k], s_lo.at[k], r_hi.at[k],
            device_id=(ix - 1, iy), device_id_type=MESH)

    def to_right(k):
        return pltpu.make_async_remote_copy(
            send_hi.at[k], recv_lo.at[k], s_hi.at[k], r_lo.at[k],
            device_id=(ix + 1, iy), device_id_type=MESH)

    h_left = pltpu.make_async_remote_copy(
        hx.at[8:16], hx.at[8 + cols : 16 + cols], hs_sem.at[0], hr_sem.at[1],
        device_id=(ix - 1, iy), device_id_type=MESH)
    h_right = pltpu.make_async_remote_copy(
        hx.at[cols : 8 + cols], hx.at[0:8], hs_sem.at[1], hr_sem.at[0],
        device_id=(ix + 1, iy), device_id_type=MESH)
    y_down = pltpu.make_async_remote_copy(
        q_ref.at[:, :, 0:128], above, ys_sem.at[0], yr_sem.at[1],
        device_id=(ix, iy - 1), device_id_type=MESH)
    y_up = pltpu.make_async_remote_copy(
        q_ref.at[:, :, last : last + 128], below, ys_sem.at[1], yr_sem.at[0],
        device_id=(ix, iy + 1), device_id_type=MESH)

    def top_to(d):
        return pltpu.make_async_remote_copy(
            q_ref.at[:, :, last : last + 128], top, ts_sem.at[d], tr_sem,
            device_id=(ix, d), device_id_type=MESH)

    pack(0)
    pl.semaphore_wait(barrier, count)

    @pl.when(has_l)
    def _():
        h_left.start()
        to_left(0).start()

    @pl.when(has_r)
    def _():
        h_right.start()
        to_right(0).start()

    @pl.when(is_top)
    def _():
        for d in range(n_gy - 1):
            top_to(d).start()

    @pl.when(has_b)
    def _():
        y_down.start()

    @pl.when(has_a)
    def _():
        y_up.start()

    for k in range(1, PARTS):
        pack(k)

        @pl.when(has_l)
        def _(k=k):
            to_left(k).start()

        @pl.when(has_r)
        def _(k=k):
            to_right(k).start()

    @pl.when(jnp.logical_not(has_l))
    def _():
        hx[0:8, :] = jnp.broadcast_to(hx[8:9, :], (8, 128))
        for k in range(PARTS):
            for v in range(6):
                for g in range(groups):
                    at = (v * groups + g) * 3
                    recv_lo[k, at : at + 3, :] = jnp.broadcast_to(q_ref[v, 0:1, lanes(g, k)], (3, 128))

    @pl.when(jnp.logical_not(has_r))
    def _():
        hx[8 + cols : 16 + cols, :] = jnp.broadcast_to(hx[7 + cols : 8 + cols, :], (8, 128))
        for k in range(PARTS):
            for v in range(6):
                for g in range(groups):
                    at = (v * groups + g) * 3
                    recv_hi[k, at : at + 3, :] = jnp.broadcast_to(
                        q_ref[v, cols - 1 : cols, lanes(g, k)], (3, 128))

    for i in range(cols):
        row = bt_ref[pl.ds(sl_ref[ws_ref[i]], 1), :]
        for b in range(per_tile):
            blow[i : i + 1, b * planes : (b + 1) * planes] = row

    wide = 256
    halves = wide // 128
    height = hx[8 : 8 + cols, :]
    height_w = jnp.concatenate([height] * halves, axis=1)

    def phase_a(t, _):
        at = pl.ds(pl.multiple_of(t * wide, wide), wide)
        q = [q_ref[v, :, at] for v in range(6)]
        r, u, v, w, p, c = primitives(q)
        keep[0, :, at] = r
        keep[1, :, at] = p
        keep[2, :, at] = c
        rp = 1.0 / p
        inv_t = q[0] * rp
        eq = 3.0 / (jnp.exp(3.0 * inv_t) - 1.0)
        keep[3, :, at] = (q[0] * eq - q[5]) * p * (500.0 * jnp.exp(-jnp.exp(jnp.log(inv_t) * (1.0 / 3.0))))
        hc = height_w * c
        hp = height_w * p
        for axis, vel in ((0, u), (1, w)):
            hv = height_w * vel
            speed = jnp.abs(hv) + hc
            for n in range(6):
                flux = hv * q[n]
                if n == (1, 3)[axis]:
                    flux = flux + hp
                if n == 4:
                    flux = flux + hv * p
                for s, x in ((0, flux), (1, speed * q[n])):
                    for lo, y in enumerate(split(x)):
                        slab = s + 2 * lo
                        if axis == 0:
                            rx[pl.ds((slab * 6 + n) * cols, cols), at] = y
                        else:
                            for b in range(halves):
                                zs[t * halves + b, pl.ds(n * cols, cols), pl.ds(slab * 128, 128)] = (
                                    y[:, b * 128 : (b + 1) * 128])
        return 0

    lax.fori_loop(0, length // wide, phase_a, 0)

    @pl.when(has_l)
    def _():
        h_right.wait_recv()

    @pl.when(has_r)
    def _():
        h_left.wait_recv()

    @pl.when(jnp.logical_not(is_top))
    def _():
        top_to(0).wait_recv()

    @pl.when(is_top)
    def _():
        top[...] = q_ref[:, :, last : last + 128]

    slope_x = (hx[6 : 6 + cols, :] - 8.0 * hx[7 : 7 + cols, :] + 8.0 * hx[9 : 9 + cols, :]
               - hx[10 : 10 + cols, :]) / 0.6
    slope_z = (pltpu.roll(height, 2, 1) - 8.0 * pltpu.roll(height, 1, 1)
               + 8.0 * pltpu.roll(height, 127, 1) - pltpu.roll(height, 126, 1)) / 0.6
    for v in range(6):
        for b in range(per_tile - 1):
            top[v, :, b * planes : (b + 1) * planes] = top[v, :, 128 - planes : 128]
    tq = [top[v] for v in range(6)]
    r, u, v, w, p, c = primitives(tq)
    slope_sq = slope_x * slope_x + slope_z * slope_z
    g2 = 1.0 + slope_sq
    g = jnp.sqrt(g2)
    pj = 0.1 * (1.0 + 2.8 / 2.4 * (36.0 * slope_x * slope_x / g2 - 1.0))
    rate = (v - u * slope_x - w * slope_z) + g * (pj - p) * r / c
    shock_ref[...] = h_ref[...] + dt * rate[:, 0:planes]

    @pl.when(has_b)
    def _():
        y_up.wait_recv()

    @pl.when(has_a)
    def _():
        y_down.wait_recv()

    @pl.when(jnp.logical_not(has_b))
    def _():
        for v in range(6):
            for b in range(per_tile):
                below[v, :, b * planes : (b + 1) * planes] = (
                    q_ref[v, :, 128 - (b + 1) * planes : 128 - b * planes])
        old = below[2]
        blown = 2.0 * blow[...] - old
        below[2] = blown
        below[4] = below[4] + 0.5 * (blown * blown - old * old) / below[0]

    @pl.when(is_top)
    def _():
        above[...] = top[...]

    first_row = iy * (length // planes)

    def growth(tile, width):
        row = first_row + tile * per_tile + lax.broadcasted_iota(jnp.int32, (1, width), 1) // planes
        return jnp.exp(2.0 * (row.astype(F32) + 0.5) / total_rows)

    def y_flux(tile, width, q, u, v, w, p, c):
        reps = width // 128
        def rep(x):
            return x if reps == 1 else jnp.concatenate([x] * reps, axis=1)
        eta = (growth(tile, width) - 1.0) * (1.0 / DEN)
        kx, kz, kt = -eta * rep(slope_x), -eta * rep(slope_z), -eta * rep(rate)
        uc = kt + kx * u + v + kz * w
        nrm = 1.0 + eta * eta * rep(slope_sq)
        speed = jnp.abs(uc) + c * (nrm * lax.rsqrt(nrm))
        extra = {1: kx * p, 2: p, 3: kz * p, 4: p * (uc - kt)}
        for n in range(6):
            flux = q[n] * uc
            if n in extra:
                flux = flux + extra[n]
            for s, x in ((0, flux), (1, speed * q[n])):
                for lo, y in enumerate(split(x)):
                    slab = s + 2 * lo
                    for b in range(reps):
                        ys[tile + 1 + b, pl.ds(n * cols, cols), pl.ds(slab * 128, 128)] = (
                            y[:, b * 128 : (b + 1) * 128])

    for ref, tile in ((below, -1), (above, tiles)):
        gq = [ref[v] for v in range(6)]
        gr, gu, gv, gw, gp, gc = primitives(gq)
        y_flux(tile, 128, gq, gu, gv, gw, gp, gc)

    def phase_b(t, _):
        at = pl.ds(pl.multiple_of(t * wide, wide), wide)
        q = [q_ref[v, :, at] for v in range(6)]
        r, p, c = keep[0, :, at], keep[1, :, at], keep[2, :, at]
        y_flux(t * halves, wide, q, q[1] * r, q[2] * r, q[3] * r, p, c)
        return 0

    lax.fori_loop(0, length // wide, phase_b, 0)

    for m in mats:
        m.wait()

    inv_h = 1.0 / height
    scale = (-dt / 3.0) * inv_h
    decay = dt * rate * inv_h
    span = 4

    def dot(a, b):
        return jnp.dot(a, b, preferred_element_type=F32)

    def phase_c(gidx, _):
        t0 = gidx * span
        dx = dot(mx[...], rx[:, pl.ds(pl.multiple_of(t0 * 128, 128 * span), 128 * span)])
        dz = dot(zs[pl.ds(t0, span)].reshape(span * 6 * cols, 512), mz[...])
        dy = dot(ys[pl.ds(t0, span)].reshape(span * 6 * cols, 512), my[0])
        dy = dy + dot(ys[pl.ds(t0 + 1, span)].reshape(span * 6 * cols, 512), my[1])
        dy = dy + dot(ys[pl.ds(t0 + 2, span)].reshape(span * 6 * cols, 512), my[2])
        for b in range(span):
            at = pl.ds(pl.multiple_of((t0 + b) * 128, 128), 128)
            wy = (0.05 * total_rows * DEN / 2.0) / growth(t0 + b, 128)
            for v in range(6):
                lo = (b * 6 + v) * cols
                q = q_ref[v, :, at]
                d = dx[v * cols : (v + 1) * cols, b * 128 : (b + 1) * 128]
                d = d + dz[lo : lo + cols] + wy * dy[lo : lo + cols]
                new = q + scale * d - q * decay
                if v == 5:
                    new = new + dt * keep[3, :, at]
                out_ref[v, :, at] = new
        return 0

    lax.fori_loop(0, tiles // span, phase_c, 0)

    hl, hh = hx[5:8, :], hx[8 + cols : 11 + cols, :]
    heights = [jnp.concatenate([x] * groups, axis=0) for x in (hl, hh)]
    size = groups * 3
    for k in range(PARTS):
        @pl.when(has_l)
        def _(k=k):
            to_right(k).wait_recv()

        @pl.when(has_r)
        def _(k=k):
            to_left(k).wait_recv()

        for side, ref in enumerate((recv_lo, recv_hi)):
            q = [ref[k, v * size : (v + 1) * size, :] for v in range(6)]
            r, u, v, w, p, c = primitives(q)
            hv = heights[side] * u
            speed = jnp.abs(hv) + heights[side] * c
            for n in range(6):
                flux = hv * q[n]
                if n == 1:
                    flux = flux + heights[side] * p
                if n == 4:
                    flux = flux + hv * p
                fs, as_ = split(flux), split(speed * q[n])
                block = jnp.concatenate([fs[0].astype(F32), as_[0].astype(F32), fs[1].astype(F32), as_[1].astype(F32)], axis=0).astype(BF16)
                rh[side * 4 * size : (side + 1) * 4 * size, n * 128 : (n + 1) * 128] = block
        d = dot(mh[...], rh[...])
        for g in range(groups):
            for v in range(6):
                out_ref[v, :, lanes(g, k)] += scale * d[g * cols : (g + 1) * cols, v * 128 : (v + 1) * 128]

    @pl.when(has_l)
    def _():
        h_left.wait_send()
        for k in range(PARTS):
            to_left(k).wait_send()

    @pl.when(has_r)
    def _():
        h_right.wait_send()
        for k in range(PARTS):
            to_right(k).wait_send()

    @pl.when(is_top)
    def _():
        for d in range(n_gy - 1):
            top_to(d).wait_send()

    @pl.when(has_b)
    def _():
        y_down.wait_send()

    @pl.when(has_a)
    def _():
        y_up.wait_send()


def solution(mesh):
    n_gx, n_gy = mesh.shape["gx"], mesh.shape["gy"]

    def shards(state, shock_height, wall_segment, segment_level, blow_table):
        planes = blow_table.shape[1]
        cols, length = state.shape[1], state.shape[2]
        tiles = length // 128
        groups = tiles // PARTS
        mats = [jnp.asarray(m, BF16) for m in stencil_matrices(cols, planes)]
        vmem = pl.BlockSpec(memory_space=pltpu.VMEM)
        smem = pl.BlockSpec(memory_space=pltpu.SMEM)
        hbm = pl.BlockSpec(memory_space=pl.ANY)
        packed = pltpu.VMEM((PARTS, 18 * groups, 128), F32)
        tile6 = pltpu.VMEM((6, cols, 128), F32)
        sem = pltpu.SemaphoreType.DMA
        return pl.pallas_call(
            functools.partial(kernel, n_gx, n_gy, planes),
            out_shape=(
                jax.ShapeDtypeStruct(state.shape, F32),
                jax.ShapeDtypeStruct(shock_height.shape, F32),
            ),
            in_specs=[vmem, vmem, smem, smem, vmem, hbm, hbm, hbm, hbm],
            out_specs=(vmem, vmem),
            scratch_shapes=[
                packed, packed, packed, packed,
                pltpu.VMEM((16 + cols, 128), F32),
                tile6, tile6, tile6,
                pltpu.VMEM((24 * cols, length), BF16),
                pltpu.VMEM((tiles, 6 * cols, 512), BF16),
                pltpu.VMEM((tiles + 2, 6 * cols, 512), BF16),
                pltpu.VMEM((4, cols, length), F32),
                pltpu.VMEM((24 * groups, 768), BF16),
                *[pltpu.VMEM(m.shape, BF16) for m in mats],
                pltpu.VMEM((cols, 128), F32),
                sem((4,)), sem((PARTS,)), sem((PARTS,)), sem((PARTS,)), sem((PARTS,)),
                sem((2,)), sem((2,)), sem((2,)), sem((2,)), sem((n_gy,)), sem,
            ],
            compiler_params=pltpu.CompilerParams(
                collective_id=0, has_side_effects=True, vmem_limit_bytes=40 * 1024 * 1024),
        )(state, shock_height, wall_segment, segment_level, blow_table, *mats)

    in_specs = (P(None, "gx", "gy"), P("gx", None), P("gx"), P(), P())
    out_specs = (P(None, "gx", "gy"), P("gx", None))
    return jax.shard_map(shards, mesh=mesh, in_specs=in_specs, out_specs=out_specs, check_vma=False)
```

time: 98.1 us -> 27 us (0.28)
  the two profiles are of different devices: /device:TPU:9 before, /device:TPU:10 now
where the time goes in v1:
time: 27 us; the launch traced here: 26.6 us
  Pallas kernels  16.7 us (62%)
  local copies, waits for them, and re-layouts  9.2 us (34%)
  between operations  0.66 us (2%)
    pallas_call x1, Pallas kernels, shards(): pl.pallas_call(functools.partial(kernel, n_gx, n_gy, planes), out_shape=(...  16.7 us
    unnamed x20, local copies, waits for them, and re-layouts  9.2 us

profile of v1, /device:TPU:10, one launch (start us, length us, event | category | flops | bytes accessed | tf_op | source)
XLA Modules:
  0.0 26.6 jit_solution(17553317444560461670)
XLA Ops:
  0.6 0.0 copy-start
  0.6 1.3 %copy-done = f32[6,16,3072]{2,1,0:T(8,128)S(1)} copy-done((f32[6,16,3072]{2,1,0:T(8,128)S(1)}, f32[6,16,3072]{2,1,0:T(8,128)}, u32[]{:S(2)}) %copy-start) | copy-done | bytes 1179672
  1.9 0.0 copy-start.1
  1.9 1.0 %copy-done.1 = bf16[3,512,128]{2,1,0:T(8,128)(2,1)S(1)} copy-done((bf16[3,512,128]{2,1,0:T(8,128)(2,1)S(1)}, bf16[3,512,128]{2,1,0:T(8,128)(2,1)}, u32[]{:S(2)}) %copy-start.1) | copy-done | bytes 393240
  2.9 0.0 copy-start.2
  2.9 0.9 %copy-done.2 = bf16[512,128]{1,0:T(8,128)(2,1)S(1)} copy-done((bf16[512,128]{1,0:T(8,128)(2,1)S(1)}, bf16[512,128]{1,0:T(8,128)(2,1)}, u32[]{:S(2)}) %copy-start.2) | copy-done | bytes 131096
  3.8 0.0 copy-start.3
  3.8 0.9 %copy-done.3 = bf16[96,384]{1,0:T(8,128)(2,1)S(1)} copy-done((bf16[96,384]{1,0:T(8,128)(2,1)S(1)}, bf16[96,384]{1,0:T(8,128)(2,1)}, u32[]{:S(2)}) %copy-start.3) | copy-done | bytes 73752
  4.7 0.0 copy-start.4
  4.7 0.8 %copy-done.4 = bf16[128,192]{1,0:T(8,128)(2,1)S(1)} copy-done((bf16[128,192]{1,0:T(8,128)(2,1)S(1)}, bf16[128,192]{1,0:T(8,128)(2,1)}, u32[]{:S(2)}) %copy-start.4) | copy-done | bytes 49176
  5.5 0.0 copy-start.5
  5.5 0.7 %copy-done.5 = f32[16,32]{1,0:T(8,128)S(1)} copy-done((f32[16,32]{1,0:T(8,128)S(1)}, f32[16,32]{1,0:T(8,128)}, u32[]{:S(2)}) %copy-start.5) | copy-done | bytes 2072
  6.2 0.0 copy-start.6
  6.2 0.7 %copy-done.6 = f32[16,32]{1,0:T(8,128)S(1)} copy-done((f32[16,32]{1,0:T(8,128)S(1)}, f32[16,32]{1,0:T(8,128)}, u32[]{:S(2)}) %copy-start.6) | copy-done | bytes 2072
  6.9 0.0 copy-start.7
  6.9 0.7 %copy-done.7 = s32[16]{0:T(128)S(1)} copy-done((s32[16]{0:T(128)S(1)}, s32[16]{0:T(128)}, u32[]{:S(2)}) %copy-start.7) | copy-done | bytes 88
  7.6 0.0 copy-start.8
  7.6 0.7 %copy-done.8 = s32[16]{0:T(128)S(1)} copy-done((s32[16]{0:T(128)S(1)}, s32[16]{0:T(128)}, u32[]{:S(2)}) %copy-start.8) | copy-done | bytes 88
  8.2 16.7 %shard_map.104 = (f32[6,16,3072]{2,1,0:T(8,128)S(1)}, f32[16,32]{1,0:T(8,128)S(1)}) custom-call(f32[6,16,3072]{2,1,0:T(8,128)S(1)} %copy-done, f32[16,32]{1,0:T(8,128)S(1)} %copy-done.5, s32[16]{0:T(128)S(1)} %copy-done.7, s32[16]{0:T(128)S(1)} %copy-done.8, f32[16,32]{1,0:T(8,128)S(1)} %copy-done.6, bf16[96,384]{1,0:T(8,128)(2,1)S(1)} %copy-done.3, ...), custom_call_target="tpu_custom_call" | custom-call | tf_op jit(solution)/shard_map/pallas_call | solution.py:459
  25.0 1.0 %copy.13 = f32[6,16,3072]{2,1,0:T(8,128)} copy(f32[6,16,3072]{2,1,0:T(8,128)S(1)} %get-tuple-element.4) | data formatting | bytes 2359296
  26.0 0.6 %copy.14 = f32[16,32]{1,0:T(8,128)} copy(f32[16,32]{1,0:T(8,128)S(1)} %get-tuple-element.5) | data formatting | bytes 4096
Async XLA Ops:
  0.6 1.3 %copy-start = (f32[6,16,3072]{2,1,0:T(8,128)S(1)}, f32[6,16,3072]{2,1,0:T(8,128)}, u32[]{:S(2)}) copy-start(f32[6,16,3072]{2,1,0:T(8,128)} %q_ref.1) | copy-start | bytes 3538948
  1.9 1.0 %copy-start.1 = (bf16[3,512,128]{2,1,0:T(8,128)(2,1)S(1)}, bf16[3,512,128]{2,1,0:T(8,128)(2,1)}, u32[]{:S(2)}) copy-start(bf16[3,512,128]{2,1,0:T(8,128)(2,1)} %constant.10.clone.my_hbm) | copy-start | bytes 1179652
  2.9 0.9 %copy-start.2 = (bf16[512,128]{1,0:T(8,128)(2,1)S(1)}, bf16[512,128]{1,0:T(8,128)(2,1)}, u32[]{:S(2)}) copy-start(bf16[512,128]{1,0:T(8,128)(2,1)} %constant.9.clone.mz_hbm) | copy-start | bytes 393220
  3.8 0.9 %copy-start.3 = (bf16[96,384]{1,0:T(8,128)(2,1)S(1)}, bf16[96,384]{1,0:T(8,128)(2,1)}, u32[]{:S(2)}) copy-start(bf16[96,384]{1,0:T(8,128)(2,1)} %constant.8.clone.mx_hbm) | copy-start | bytes 221188
  4.7 0.8 %copy-start.4 = (bf16[128,192]{1,0:T(8,128)(2,1)S(1)}, bf16[128,192]{1,0:T(8,128)(2,1)}, u32[]{:S(2)}) copy-start(bf16[128,192]{1,0:T(8,128)(2,1)} %constant.11.clone.mh_hbm) | copy-start | bytes 147460
  5.5 0.7 %copy-start.5 = (f32[16,32]{1,0:T(8,128)S(1)}, f32[16,32]{1,0:T(8,128)}, u32[]{:S(2)}) copy-start(f32[16,32]{1,0:T(8,128)} %h_ref.1) | copy-start | bytes 6148
  6.2 0.7 %copy-start.6 = (f32[16,32]{1,0:T(8,128)S(1)}, f32[16,32]{1,0:T(8,128)}, u32[]{:S(2)}) copy-start(f32[16,32]{1,0:T(8,128)} %bt_ref.1) | copy-start | bytes 6148
  6.9 0.7 %copy-start.7 = (s32[16]{0:T(128)S(1)}, s32[16]{0:T(128)}, u32[]{:S(2)}) copy-start(s32[16]{0:T(128)} %ws_ref.1) | copy-start | bytes 196
  7.6 0.7 %copy-start.8 = (s32[16]{0:T(128)S(1)}, s32[16]{0:T(128)}, u32[]{:S(2)}) copy-start(s32[16]{0:T(128)} %sl_ref.1) | copy-start | bytes 196

commit v2 on v1

--- a/solution.py
+++ b/solution.py
@@ -68,13 +68,14 @@
 
 def kernel(
     n_gx, n_gy, planes,
-    q_ref, h_ref, ws_ref, sl_ref, bt_ref, mx_hbm, mz_hbm, my_hbm, mh_hbm,
+    q_hbm, h_hbm, ws_hbm, sl_hbm, bt_hbm, mx_hbm, mz_hbm, my_hbm, mh_hbm,
     out_ref, shock_ref,
+    q_ref, h_ref, ws_ref, sl_ref, bt_ref,
     send_lo, send_hi, recv_lo, recv_hi, hx, below, above, top,
     rx, zs, ys, keep, rh, mx, mz, my, mh, blow,
     mat_sem, s_lo, s_hi, r_lo, r_hi, hs_sem, hr_sem, ys_sem, yr_sem, ts_sem, tr_sem,
 ):
-    cols, length = q_ref.shape[1], q_ref.shape[2]
+    cols, length = q_hbm.shape[1], q_hbm.shape[2]
     tiles = length // 128
     per_tile = 128 // planes
     total_rows = n_gy * (length // planes)
@@ -88,9 +89,11 @@
 
     mats = [
         pltpu.make_async_copy(a, b, mat_sem.at[i])
-        for i, (a, b) in enumerate(((mx_hbm, mx), (mz_hbm, mz), (my_hbm, my), (mh_hbm, mh)))
+        for i, (a, b) in enumerate((
+            (q_hbm, q_ref), (h_hbm, h_ref), (ws_hbm, ws_ref), (sl_hbm, sl_ref), (bt_hbm, bt_ref),
+            (mx_hbm, mx), (mz_hbm, mz), (my_hbm, my), (mh_hbm, mh)))
     ]
-    for m in mats:
+    for m in mats[:2]:
         m.start()
 
     barrier = pltpu.get_barrier_semaphore()
@@ -111,6 +114,11 @@
         @pl.when(near)
         def _(d=d):
             pl.semaphore_signal(barrier, inc=1, device_id=(ix, d), device_id_type=MESH)
+
+    for m in mats[2:]:
+        m.start()
+    for m in mats[:2]:
+        m.wait()
 
     for b in range(per_tile):
         hx[8 : 8 + cols, b * planes : (b + 1) * planes] = h_ref[...]
@@ -208,6 +216,9 @@
                     at = (v * groups + g) * 3
                     recv_hi[k, at : at + 3, :] = jnp.broadcast_to(
                         q_ref[v, cols - 1 : cols, lanes(g, k)], (3, 128))
+
+    for m in mats[2:5]:
+        m.wait()
 
     for i in range(cols):
         row = bt_ref[pl.ds(sl_ref[ws_ref[i]], 1), :]
@@ -350,7 +361,7 @@
 
     lax.fori_loop(0, length // wide, phase_b, 0)
 
-    for m in mats:
+    for m in mats[5:]:
         m.wait()
 
     inv_h = 1.0 / height
@@ -451,8 +462,7 @@
         groups = tiles // PARTS
         mats = [jnp.asarray(m, BF16) for m in stencil_matrices(cols, planes)]
         vmem = pl.BlockSpec(memory_space=pltpu.VMEM)
-        smem = pl.BlockSpec(memory_space=pltpu.SMEM)
-        hbm = pl.BlockSpec(memory_space=pl.ANY)
+        hbm = pl.BlockSpec(memory_space=pltpu.HBM)
         packed = pltpu.VMEM((PARTS, 18 * groups, 128), F32)
         tile6 = pltpu.VMEM((6, cols, 128), F32)
         sem = pltpu.SemaphoreType.DMA
@@ -462,9 +472,14 @@
                 jax.ShapeDtypeStruct(state.shape, F32),
                 jax.ShapeDtypeStruct(shock_height.shape, F32),
             ),
-            in_specs=[vmem, vmem, smem, smem, vmem, hbm, hbm, hbm, hbm],
+            in_specs=[hbm] * 9,
             out_specs=(vmem, vmem),
             scratch_shapes=[
+                pltpu.VMEM(state.shape, F32),
+                pltpu.VMEM(shock_height.shape, F32),
+                pltpu.SMEM(wall_segment.shape, jnp.int32),
+                pltpu.SMEM(segment_level.shape, jnp.int32),
+                pltpu.VMEM(blow_table.shape, F32),
                 packed, packed, packed, packed,
                 pltpu.VMEM((16 + cols, 128), F32),
                 tile6, tile6, tile6,
@@ -475,11 +490,11 @@
                 pltpu.VMEM((24 * groups, 768), BF16),
                 *[pltpu.VMEM(m.shape, BF16) for m in mats],
                 pltpu.VMEM((cols, 128), F32),
-                sem((4,)), sem((PARTS,)), sem((PARTS,)), sem((PARTS,)), sem((PARTS,)),
+                sem((9,)), sem((PARTS,)), sem((PARTS,)), sem((PARTS,)), sem((PARTS,)),
                 sem((2,)), sem((2,)), sem((2,)), sem((2,)), sem((n_gy,)), sem,
             ],
             compiler_params=pltpu.CompilerParams(
-                collective_id=0, has_side_effects=True, vmem_limit_bytes=40 * 1024 * 1024),
+                collective_id=0, has_side_effects=True, vmem_limit_bytes=62 * 1024 * 1024),
         )(state, shock_height, wall_segment, segment_level, blow_table, *mats)
 
     in_specs = (P(None, "gx", "gy"), P("gx", None), P("gx"), P(), P())

time: 27 us -> 20.5 us (0.76)
  local copies, waits for them, and re-layouts: 9.2 us -> 2.97 us
    unnamed x20 -> x4, local copies, waits for them, and re-layouts: 9.2 us -> 2.97 us
where the time goes in v2:
time: 20.5 us; the launch traced here: 20.3 us
  Pallas kernels  16.7 us (81%)
  local copies, waits for them, and re-layouts  2.97 us (14%)
  between operations  0.65 us (3%)
    pallas_call x1, Pallas kernels, shards(): pl.pallas_call(functools.partial(kernel, n_gx, n_gy, planes), out_shape=(...  16.7 us
    unnamed x4, local copies, waits for them, and re-layouts  2.97 us

profile of v2, /device:TPU:10, one launch (start us, length us, event | category | flops | bytes accessed | tf_op | source)
XLA Modules:
  0.0 20.3 jit_solution(5374879735799370836)
XLA Ops:
  0.6 16.7 %shard_map.104 = (f32[6,16,3072]{2,1,0:T(8,128)}, f32[16,32]{1,0:T(8,128)}) custom-call(f32[6,16,3072]{2,1,0:T(8,128)} %q_hbm.1, f32[16,32]{1,0:T(8,128)} %h_hbm.1, s32[16]{0:T(128)} %ws_hbm.1, s32[16]{0:T(128)} %sl_hbm.1, f32[16,32]{1,0:T(8,128)} %bt_hbm.1, bf16[96,384]{1,0:T(8,128)(2,1)} %constant.8.clone.mx_hbm, bf16[512,128]{1,0:T(8,128)(2,1)} %constant.9.clone.mz_hbm, ...), custom_call_target="tpu_custom_call" | custom-call | tf_op jit(solution)/shard_map/pallas_call | solution.py:469
  17.3 0.0 copy-start
  17.3 2.4 %copy.13 = f32[6,16,3072]{2,1,0:T(8,128)} copy(f32[6,16,3072]{2,1,0:T(8,128)} %get-tuple-element.4) | data formatting | bytes 2359296
  19.7 0.0 copy-done
  19.7 0.6 %copy.14 = f32[16,32]{1,0:T(8,128)} copy(f32[16,32]{1,0:T(8,128)S(1)} %copy-done) | data formatting | bytes 4096
Async XLA Ops:
  17.3 2.4 %copy-start = (f32[16,32]{1,0:T(8,128)S(1)}, f32[16,32]{1,0:T(8,128)}, u32[]{:S(2)}) copy-start(f32[16,32]{1,0:T(8,128)} %get-tuple-element.5) | copy-start | bytes 6148

commit v3 on v2

--- a/solution.py
+++ b/solution.py
@@ -69,11 +69,11 @@
 def kernel(
     n_gx, n_gy, planes,
     q_hbm, h_hbm, ws_hbm, sl_hbm, bt_hbm, mx_hbm, mz_hbm, my_hbm, mh_hbm,
-    out_ref, shock_ref,
-    q_ref, h_ref, ws_ref, sl_ref, bt_ref,
+    out_hbm, shock_ref,
+    out_ref, q_ref, h_ref, ws_ref, sl_ref, bt_ref,
     send_lo, send_hi, recv_lo, recv_hi, hx, below, above, top,
     rx, zs, ys, keep, rh, mx, mz, my, mh, blow,
-    mat_sem, s_lo, s_hi, r_lo, r_hi, hs_sem, hr_sem, ys_sem, yr_sem, ts_sem, tr_sem,
+    mat_sem, out_sem, s_lo, s_hi, r_lo, r_hi, hs_sem, hr_sem, ys_sem, yr_sem, ts_sem, tr_sem,
 ):
     cols, length = q_hbm.shape[1], q_hbm.shape[2]
     tiles = length // 128
@@ -398,6 +398,11 @@
     hl, hh = hx[5:8, :], hx[8 + cols : 11 + cols, :]
     heights = [jnp.concatenate([x] * groups, axis=0) for x in (hl, hh)]
     size = groups * 3
+
+    def write(g, k):
+        return pltpu.make_async_copy(
+            out_ref.at[:, :, lanes(g, k)], out_hbm.at[:, :, lanes(g, k)], out_sem.at[k, g])
+
     for k in range(PARTS):
         @pl.when(has_l)
         def _(k=k):
@@ -425,6 +430,11 @@
         for g in range(groups):
             for v in range(6):
                 out_ref[v, :, lanes(g, k)] += scale * d[g * cols : (g + 1) * cols, v * 128 : (v + 1) * 128]
+            write(g, k).start()
+
+    for k in range(PARTS):
+        for g in range(groups):
+            write(g, k).wait()
 
     @pl.when(has_l)
     def _():
@@ -450,6 +460,19 @@
     @pl.when(has_a)
     def _():
         y_up.wait_send()
+
+
+def finish(a_hbm, b_hbm, x_hbm, y_hbm, a, b, in_sem, out_sem):
+    moves = [(a_hbm.at[v], a.at[v], x_hbm.at[v]) for v in range(6)] + [(b_hbm, b, y_hbm)]
+    loads = [pltpu.make_async_copy(m[0], m[1], in_sem.at[i]) for i, m in enumerate(moves)]
+    stores = [pltpu.make_async_copy(m[1], m[2], out_sem.at[i]) for i, m in enumerate(moves)]
+    for c in loads:
+        c.start()
+    for c, d in zip(loads, stores):
+        c.wait()
+        d.start()
+    for d in stores:
+        d.wait()
 
 
 def solution(mesh):
@@ -466,15 +489,16 @@
         packed = pltpu.VMEM((PARTS, 18 * groups, 128), F32)
         tile6 = pltpu.VMEM((6, cols, 128), F32)
         sem = pltpu.SemaphoreType.DMA
-        return pl.pallas_call(
+        state_out, shock_out = pl.pallas_call(
             functools.partial(kernel, n_gx, n_gy, planes),
             out_shape=(
                 jax.ShapeDtypeStruct(state.shape, F32),
                 jax.ShapeDtypeStruct(shock_height.shape, F32),
             ),
             in_specs=[hbm] * 9,
-            out_specs=(vmem, vmem),
+            out_specs=(hbm, vmem),
             scratch_shapes=[
+                pltpu.VMEM(state.shape, F32),
                 pltpu.VMEM(state.shape, F32),
                 pltpu.VMEM(shock_height.shape, F32),
                 pltpu.SMEM(wall_segment.shape, jnp.int32),
@@ -490,12 +514,27 @@
                 pltpu.VMEM((24 * groups, 768), BF16),
                 *[pltpu.VMEM(m.shape, BF16) for m in mats],
                 pltpu.VMEM((cols, 128), F32),
-                sem((9,)), sem((PARTS,)), sem((PARTS,)), sem((PARTS,)), sem((PARTS,)),
+                sem((9,)), sem((PARTS, groups)), sem((PARTS,)), sem((PARTS,)), sem((PARTS,)), sem((PARTS,)),
                 sem((2,)), sem((2,)), sem((2,)), sem((2,)), sem((n_gy,)), sem,
             ],
             compiler_params=pltpu.CompilerParams(
                 collective_id=0, has_side_effects=True, vmem_limit_bytes=62 * 1024 * 1024),
         )(state, shock_height, wall_segment, segment_level, blow_table, *mats)
+        return pl.pallas_call(
+            finish,
+            out_shape=(
+                jax.ShapeDtypeStruct(state.shape, F32),
+                jax.ShapeDtypeStruct(shock_height.shape, F32),
+            ),
+            in_specs=[hbm, hbm],
+            out_specs=(hbm, hbm),
+            scratch_shapes=[
+                pltpu.VMEM(state.shape, F32),
+                pltpu.VMEM(shock_height.shape, F32),
+                sem((7,)), sem((7,)),
+            ],
+            compiler_params=pltpu.CompilerParams(vmem_limit_bytes=62 * 1024 * 1024),
+        )(state_out, shock_out)
 
     in_specs = (P(None, "gx", "gy"), P("gx", None), P("gx"), P(), P())
     out_specs = (P(None, "gx", "gy"), P("gx", None))

time: 20.5 us -> 20.3 us (level)
  local copies, waits for them, and re-layouts: 2.97 us -> 0 us
  Pallas kernels: 16.7 us -> 19.5 us
    unnamed x4 -> x0, local copies, waits for them, and re-layouts: 2.97 us -> none
    pallas_call x0 -> x1, Pallas kernels: none -> 2.15 us  [shards(): pl.pallas_call(finish, out_shape=(jax.ShapeDtypeStruct(state.shape, F32),...]
    pallas_call x1, Pallas kernels: 16.7 us -> 17.3 us  [shards(): pl.pallas_call(functools.partial(kernel, n_gx, n_gy, planes), out_shape=(...]
where the time goes in v3:
time: 20.3 us; the launch traced here: 20.1 us
  Pallas kernels  19.5 us (96%)
  between operations  0.64 us (3%)
    pallas_call x1, Pallas kernels, shards(): pl.pallas_call(functools.partial(kernel, n_gx, n_gy, planes), out_shape=(...  17.3 us
    pallas_call x1, Pallas kernels, shards(): pl.pallas_call(finish, out_shape=(jax.ShapeDtypeStruct(state.shape, F32),...  2.15 us

profile of v3, /device:TPU:10, one launch (start us, length us, event | category | flops | bytes accessed | tf_op | source)
XLA Modules:
  0.0 20.1 jit_solution(13527502979250171854)
XLA Ops:
  0.6 17.3 %shard_map.104 = (f32[6,16,3072]{2,1,0:T(8,128)}, f32[16,32]{1,0:T(8,128)}) custom-call(f32[6,16,3072]{2,1,0:T(8,128)} %q_hbm.1, f32[16,32]{1,0:T(8,128)} %h_hbm.1, s32[16]{0:T(128)} %ws_hbm.1, s32[16]{0:T(128)} %sl_hbm.1, f32[16,32]{1,0:T(8,128)} %bt_hbm.1, bf16[96,384]{1,0:T(8,128)(2,1)} %constant.8.clone.mx_hbm, bf16[512,128]{1,0:T(8,128)(2,1)} %constant.9.clone.mz_hbm, ...), custom_call_target="tpu_custom_call" | custom-call | tf_op jit(solution)/shard_map/pallas_call | solution.py:492
  17.9 2.1 %shard_map.105 = (f32[6,16,3072]{2,1,0:T(8,128)}, f32[16,32]{1,0:T(8,128)}) custom-call(f32[6,16,3072]{2,1,0:T(8,128)} %get-tuple-element.4.a_hbm, f32[16,32]{1,0:T(8,128)} %get-tuple-element.5.b_hbm), custom_call_target="tpu_custom_call" | custom-call | tf_op jit(solution)/shard_map/pallas_call | solution.py:523
